TPU v7x, 32 devices: a whole 2x2x4 slice. The times are simulated.
32 devices in a mesh: region: 4 (over x, core), dom: 8 (over z, y).
Axes of the slice: x: 2, y: 2, z: 4, core: 2. Of those that a mesh axis runs over, the one named last changes fastest.
Arguments:
- x_init: bfloat16 [131072, 128], P(('region', 'dom')), may hold values from -6 to 6
- tiles: bfloat16 [9216, 128, 128], P(('region', 'dom'))
- tile_row: int32 [9216], P(('region', 'dom')), may hold values from 0 to 31
- tile_col: int32 [9216], P(('region', 'dom')), may hold values from 0 to 63, as said below
- send_list: int32 [32, 4, 8], P(('region', 'dom')), may hold values from 0 to 31, as said below
- send_count: int32 [32, 4], P(('region', 'dom')), may hold values from 1 to 8, as said below
Outputs:
- basis: bfloat16 [131072, 128], P(('region', 'dom'))
- ritz_matrix: float32 [2, 128, 128], replicated
Inputs may be any that keep to these rules, and one draw needn't show every extreme that they name: `send_list`: the 8 entries of one partition and direction are distinct row tiles of that partition. `send_count`: some partition sends 8 row tiles in every direction. `tile_col`: a value 32 + d * 8 + s with d = 0 .. 3 names slot s of the d-th received stack of extended, and s is below the count that this neighbour sends; no value names a stack where the neighbour does not exist.
All inputs are finite; a program needn't handle non-finite values.
Results may differ from a plain program's by a relative error of at most 0.00115.
The roundings to bfloat16 on the way count: a program that leaves them out, or rounds other values in their place, can miss the bound.
Values may be sent and summed in bfloat16 or wider, within the bound.
A program may use at most 64 MiB of HBM per device.

v0:
```python
import math

import jax
import jax.numpy as jnp
from jax import lax
from jax.sharding import PartitionSpec as P

ITERS = 2


HIGH = lax.Precision.HIGHEST


def padded(block, sides, width):
    for axis, dim in sides:
        count = lax.axis_size(axis)
        forward = [(i, i + 1) for i in range(count - 1)]
        backward = [(target, source) for source, target in forward]
        low = lax.ppermute(
            lax.slice_in_dim(block, block.shape[dim] - width, None, axis=dim), axis, forward
        )
        high = lax.ppermute(lax.slice_in_dim(block, 0, width, axis=dim), axis, backward)
        block = jnp.concatenate([low, block, high], axis=dim)
    return block


def local_gram(current, node_total):
    return (
        lax.dot_general(
            current, current, (((0,), (0,)), ((), ())), preferred_element_type=jnp.float32
        )
        / node_total
    )


def rayleigh_sum(partial_value):
    return lax.psum(partial_value, ("region", "dom"))


def apply_graph(basis, tiles, tile_row, tile_col, send_rows, live_slot, row_tiles, tile_size):
    vectors = basis.shape[1]
    blocks = basis.reshape(row_tiles, tile_size, vectors)
    picked = blocks[send_rows]
    packed = jnp.where(live_slot[:, :, None, None], picked, jnp.zeros_like(picked))
    along_dom = padded(jnp.stack([packed[1], packed[0]]), (("dom", 0),), 1)
    along_region = padded(jnp.stack([packed[3], packed[2]]), (("region", 0),), 1)
    received = [along_dom[0], along_dom[3], along_region[0], along_region[3]]
    extended = jnp.concatenate([blocks] + received, axis=0)
    group = 32
    group_count = tiles.shape[0] // group
    tile_groups = tiles.reshape(group_count, group, tile_size, tile_size)
    col_groups = tile_col.reshape(group_count, group)
    row_groups = tile_row.reshape(group_count, group)
    row_ids = jnp.arange(row_tiles, dtype=jnp.int32)

    def add_group(accumulated, pieces):
        tile_part, col_part, row_part = pieces
        gathered = extended[col_part]
        products = lax.dot_general(
            tile_part, gathered, (((2,), (1,)), ((0,), (0,))), preferred_element_type=jnp.float32
        )
        select = (row_part[None, :] == row_ids[:, None]).astype(jnp.float32)
        return (accumulated + jnp.einsum("rt,tiw->riw", select, products, precision=HIGH), None)

    start = jnp.zeros((row_tiles, tile_size, vectors), jnp.float32)
    applied, _ = lax.scan(add_group, start, (tile_groups, col_groups, row_groups))
    return applied.reshape(row_tiles * tile_size, vectors)


def shards(x_init, tiles, tile_row, tile_col, send_list, send_count):
    row_count, vectors = x_init.shape
    tile_size = tiles.shape[1]
    row_tiles = row_count // tile_size
    capacity = send_list.shape[2]
    node_total = row_count * lax.axis_size("region") * lax.axis_size("dom")
    root_total = math.sqrt(node_total)
    send_rows = send_list[0]
    live_slot = jnp.arange(capacity, dtype=jnp.int32)[None, :] < send_count[0][:, None]
    identity = jnp.eye(vectors, dtype=jnp.float32)
    current = x_init
    gram = lax.psum(local_gram(current, node_total), ("region", "dom"))
    rayleigh_list = []
    basis = x_init
    for iteration in range(ITERS):
        factor = jnp.linalg.cholesky(gram)
        inverse = lax.linalg.triangular_solve(factor, identity, left_side=True, lower=True)
        basis = jnp.dot(current.astype(jnp.float32), inverse.T, precision=HIGH).astype(jnp.bfloat16)
        applied = apply_graph(
            basis, tiles, tile_row, tile_col, send_rows, live_slot, row_tiles, tile_size
        )
        partial_value = jnp.dot(basis.astype(jnp.float32).T, applied, precision=HIGH) / root_total
        if iteration + 1 < ITERS:
            current = applied.astype(jnp.bfloat16)
            rayleigh_list.append(rayleigh_sum(partial_value))
            gram = lax.psum(local_gram(current, node_total), ("region", "dom"))
        else:
            rayleigh_list.append(rayleigh_sum(partial_value))
    return (basis, jnp.stack(rayleigh_list))


def solution(mesh):
    in_specs = (
        P(("region", "dom"), None),
        P(("region", "dom"), None, None),
        P(("region", "dom")),
        P(("region", "dom")),
        P(("region", "dom"), None, None),
        P(("region", "dom"), None),
    )
    out_specs = (P(("region", "dom"), None), P())
    return jax.shard_map(shards, mesh=mesh, in_specs=in_specs, out_specs=out_specs, check_vma=False)
```

profile of v0, /device:TPU:0, one launch (start us, length us, event | category | flops | bytes accessed | tf_op | source)
XLA Modules:
  0.0 653.8 jit_solution(2542297359014562458)
XLA Ops:
  9.8 124.7 %all-reduce.5.cloned.1.call-done = f32[128,128]{0,1:T(8,128)} async-done(((f32[128,128]{0,1:T(8,128)}), f32[128,128]{0,1:T(8,128)}) %all-reduce.5.cloned.1.call-update) | async-done | bytes 65552 | tf_op jit(solution)/shard_map/psum | solution.py:81
  136.3 11.7 %cholesky.44 = f32[128,128]{1,0:T(8,128)S(1)} custom-call(f32[128,128]{1,0:T(8,128)S(1)} %fusion.46), custom_call_target="Cholesky" | custom-call | tf_op jit(solution)/shard_map/jit(cholesky)/cholesky | solution.py:85
  149.3 9.8 %custom-call.8 = f32[1,128,128]{1,2,0:T(8,128)S(1)} custom-call(f32[1,128,128]{2,1,0:T(8,128)S(1)} %fusion.41), custom_call_target="InvertDiagBlocksLowerTriangular" | custom-call | tf_op jit(solution)/shard_map/triangular_solve/custom-call.0 | solution.py:86
  171.2 4.0 collective-permute-start.2
  175.3 5.1 collective-permute-done
  181.9 82.5 %while.22 = (s32[]{:T(128)}, f32[32,128,128]{2,0,1:T(8,128)}, s32[9,32]{1,0:T(8,128)S(1)}, bf16[9,32,128,128]{3,2,1,0:T(8,128)(2,1)}, s32[9,32]{1,0:T(8,128)S(1)...) while((s32[]{:T(128)}, f32[32,128,128]{2,0,1:T(8,128)}, s32[9,32]{1,0:T(8,128)S(1)}, ...), condition=%wide.region_4.7_spmd.clone, body=%wide.region_3.6_spmd.clone.sunk | while | flops 336595040 | bytes 29365292 | solution.py:66
  186.2 3.5 select_add_fusion.4
  195.3 3.5 select_add_fusion.4
  204.5 3.5 select_add_fusion.4
  213.7 3.5 select_add_fusion.4
  222.8 3.5 select_add_fusion.4
  232.0 3.5 select_add_fusion.4
  241.2 3.5 select_add_fusion.4
  250.4 3.5 select_add_fusion.4
  259.5 3.5 select_add_fusion.4
  270.6 116.5 %all-reduce.7.cloned.1.call-done = f32[128,128]{0,1:T(8,128)} async-done(((f32[128,128]{0,1:T(8,128)}), f32[128,128]{0,1:T(8,128)}) %all-reduce.7.cloned.1.call-update) | async-done | bytes 65552 | tf_op jit(solution)/shard_map/psum | solution.py:95
  388.8 11.7 %cholesky.55 = f32[128,128]{1,0:T(8,128)S(1)} custom-call(f32[128,128]{1,0:T(8,128)S(1)} %fusion.44), custom_call_target="Cholesky" | custom-call | tf_op jit(solution)/shard_map/jit(cholesky)/cholesky | solution.py:85
  401.9 9.8 %custom-call.9 = f32[1,128,128]{1,2,0:T(8,128)S(1)} custom-call(f32[1,128,128]{2,1,0:T(8,128)S(1)} %fusion.42), custom_call_target="InvertDiagBlocksLowerTriangular" | custom-call | tf_op jit(solution)/shard_map/triangular_solve/custom-call.0 | solution.py:86
  415.6 3.5 collective-permute-start.4
  423.8 4.1 collective-permute-start.6
  427.9 4.6 collective-permute-done.5
  433.9 82.3 %while.23 = (s32[]{:T(128)}, f32[32,128,128]{2,0,1:T(8,128)}, s32[9,32]{1,0:T(8,128)S(1)}, bf16[9,32,128,128]{3,2,1,0:T(8,128)(2,1)}, s32[9,32]{1,0:T(8,128)S(1)...) while((s32[]{:T(128)}, f32[32,128,128]{2,0,1:T(8,128)}, s32[9,32]{1,0:T(8,128)S(1)}, ...), condition=%wide.region_8.11_spmd.clone, body=%wide.region_7.10_spmd.clone.sunk | while | flops 336595040 | bytes 29365292 | solution.py:66
  438.2 3.5 select_add_fusion.5
  447.4 3.5 select_add_fusion.5
  456.5 3.5 select_add_fusion.5
  465.7 3.5 select_add_fusion.5
  474.8 3.5 select_add_fusion.5
  483.9 3.5 select_add_fusion.5
  493.1 3.5 select_add_fusion.5
  502.2 3.5 select_add_fusion.5
  511.4 3.5 select_add_fusion.5
  521.1 124.6 %all-reduce.9.cloned.1.call-done = (f32[1,128,128]{2,1,0:T(8,128)}, f32[1,128,128]{2,1,0:T(8,128)}) async-done(((f32[1,128,128]{2,1,0:T(8,128)}, f32[1,128,128]{2,1,0:T(8,128)}), (f32[1,128,128]{2,1,0:T(8,128)}, f32[1,128,128]{2,1,0:T(8,128)})) %all-reduce.9.cloned.1.call-update) | async-done | bytes 131088 | tf_op jit(solution)/shard_map/psum | solution.py:37
  (249 shorter events, 145.3 us)
Async XLA Ops:
  7.2 2.4 copy-start.15
  7.2 2.5 copy-start.14
  7.2 127.3 %all-reduce.5.cloned.1.call-start = ((), (), s32[]{:S(2)}) async-start(), calls=%async_computation | async-start | bytes 131072 | tf_op jit(solution)/shard_map/psum | solution.py:81
  9.5 377.5 %all-reduce.7.cloned.1.call-start = ((), (), s32[]{:S(2)}) async-start(), calls=%async_computation.1 | async-start | bytes 131072 | tf_op jit(solution)/shard_map/psum | solution.py:95
  160.4 2.3 copy-start.10
  162.8 5.6 copy-start.12
  162.8 5.7 copy-start.13
  164.9 15.4 %collective-permute-start = (bf16[1,8,128,128]{3,2,1,0:T(8,128)(2,1)}, bf16[1,8,128,128]{3,2,1,0:T(8,128)(2,1)S(1)}, u32[]{:S(2)}, u32[]{:S(2)}) collective-permute-start(bf16[1,8,128,128]{3,2,1,0:T(8,128)(2,1)} %get-tuple-element.159), channel_id=1, source_target_pairs={{0,1},{1,2},{2,3},{3,4},{4,5},{5,6},{6,7},{8,9},{9,10},{10,11},{11... | collective-permute-start | bytes 786440 | tf_op jit(solution)/shard_map/ppermute | solution.py:19
  168.5 11.9 %collective-permute-start.1 = (bf16[1,8,128,128]{3,2,1,0:T(8,128)(2,1)S(1)}, bf16[1,8,128,128]{3,2,1,0:T(8,128)(2,1)S(1)}, u32[]{:S(2)}, u32[]{:S(2)}) collective-permute-start(bf16[1,8,128,128]{3,2,1,0:T(8,128)(2,1)S(1)} %get-tuple-element.158), channel_id=1, source_target_pairs={{1,0},{2,1},{3,2},{4,3},{5,4},{6,5},{7,6},{9,8},{10,9},{11,10},{12... | collective-permute-start | bytes 786440 | tf_op jit(solution)/shard_map/ppermute | solution.py:22
  169.9 10.6 %collective-permute-start.3 = (bf16[1,8,128,128]{3,2,1,0:T(8,128)(2,1)S(1)}, bf16[1,8,128,128]{3,2,1,0:T(8,128)(2,1)S(1)}, u32[]{:S(2)}, u32[]{:S(2)}) collective-permute-start(bf16[1,8,128,128]{3,2,1,0:T(8,128)(2,1)S(1)} %get-tuple-element.156), channel_id=1, source_target_pairs={{8,0},{16,8},{24,16},{9,1},{17,9},{25,17},{10,2},{18,10},{26,18},{... | collective-permute-start | bytes 786440 | tf_op jit(solution)/shard_map/ppermute | solution.py:22
  171.2 9.2 %collective-permute-start.2 = (bf16[1,8,128,128]{3,2,1,0:T(8,128)(2,1)S(1)}, bf16[1,8,128,128]{3,2,1,0:T(8,128)(2,1)S(1)}, u32[]{:S(2)}, u32[]{:S(2)}) collective-permute-start(bf16[1,8,128,128]{3,2,1,0:T(8,128)(2,1)S(1)} %get-tuple-element.157), channel_id=1, source_target_pairs={{0,8},{8,16},{16,24},{1,9},{9,17},{17,25},{2,10},{10,18},{18,26},{... | collective-permute-start | bytes 786440 | tf_op jit(solution)/shard_map/ppermute | solution.py:19
  184.3 1.9 copy-start.1
  193.4 1.9 copy-start.1
  202.6 1.9 copy-start.1
  211.8 1.9 copy-start.1
  220.9 1.9 copy-start.1
  230.1 1.9 copy-start.1
  239.3 1.9 copy-start.1
  257.6 1.9 copy-start.1
  264.4 3.6 copy-start.3
  267.9 377.8 %all-reduce.9.cloned.1.call-start = ((), (), s32[]{:S(2)}) async-start(), calls=%async_computation.2 | async-start | bytes 262144 | tf_op jit(solution)/shard_map/psum | solution.py:37
  414.6 104.5 %copy-start.9 = (bf16[4096,128]{1,0:T(8,128)(2,1)}, bf16[4096,128]{1,0:T(8,128)(2,1)S(1)}, u32[]{:S(2)}) copy-start(bf16[4096,128]{1,0:T(8,128)(2,1)S(1)} %convolution_convert_fusion) | copy-start | bytes 3145732
  415.4 3.8 copy-start.8
  415.4 3.8 copy-start.11
  415.6 12.2 %collective-permute-start.4 = (bf16[1,8,128,128]{3,2,1,0:T(8,128)(2,1)S(1)}, bf16[1,8,128,128]{3,2,1,0:T(8,128)(2,1)S(1)}, u32[]{:S(2)}, u32[]{:S(2)}) collective-permute-start(bf16[1,8,128,128]{3,2,1,0:T(8,128)(2,1)S(1)} %get-tuple-element.155), channel_id=1, source_target_pairs={{0,1},{1,2},{2,3},{3,4},{4,5},{5,6},{6,7},{8,9},{9,10},{10,11},{11... | collective-permute-start | bytes 786440 | tf_op jit(solution)/shard_map/ppermute | solution.py:19
  421.1 11.4 %collective-permute-start.5 = (bf16[1,8,128,128]{3,2,1,0:T(8,128)(2,1)S(1)}, bf16[1,8,128,128]{3,2,1,0:T(8,128)(2,1)S(1)}, u32[]{:S(2)}, u32[]{:S(2)}) collective-permute-start(bf16[1,8,128,128]{3,2,1,0:T(8,128)(2,1)S(1)} %get-tuple-element.154), channel_id=1, source_target_pairs={{1,0},{2,1},{3,2},{4,3},{5,4},{6,5},{7,6},{9,8},{10,9},{11,10},{12... | collective-permute-start | bytes 786440 | tf_op jit(solution)/shard_map/ppermute | solution.py:22
  422.5 10.1 %collective-permute-start.7 = (bf16[1,8,128,128]{3,2,1,0:T(8,128)(2,1)S(1)}, bf16[1,8,128,128]{3,2,1,0:T(8,128)(2,1)S(1)}, u32[]{:S(2)}, u32[]{:S(2)}) collective-permute-start(bf16[1,8,128,128]{3,2,1,0:T(8,128)(2,1)S(1)} %get-tuple-element.152), channel_id=1, source_target_pairs={{8,0},{16,8},{24,16},{9,1},{17,9},{25,17},{10,2},{18,10},{26,18},{... | collective-permute-start | bytes 786440 | tf_op jit(solution)/shard_map/ppermute | solution.py:22
  423.8 8.8 %collective-permute-start.6 = (bf16[1,8,128,128]{3,2,1,0:T(8,128)(2,1)S(1)}, bf16[1,8,128,128]{3,2,1,0:T(8,128)(2,1)S(1)}, u32[]{:S(2)}, u32[]{:S(2)}) collective-permute-start(bf16[1,8,128,128]{3,2,1,0:T(8,128)(2,1)S(1)} %get-tuple-element.153), channel_id=1, source_target_pairs={{0,8},{8,16},{16,24},{1,9},{9,17},{17,25},{2,10},{10,18},{18,26},{... | collective-permute-start | bytes 786440 | tf_op jit(solution)/shard_map/ppermute | solution.py:19
  445.5 1.9 copy-start.4
  454.6 1.9 copy-start.4
  463.7 1.9 copy-start.4
  509.5 1.9 copy-start.4
  (27 other events, 39.6 us)
Sparse Core Ops, SparseCore 0:
  14.2 120.2 all-reduce.4
  268.0 118.9 all-reduce.6
  521.2 124.4 all-reduce.8
where the time goes:
time: 655 us; the launch traced here: 654 us
  waiting for transfers between devices  376 us (57%)
  matrix products  108 us (16%)
  local copies, waits for them, and re-layouts  83.8 us (13%)
  other arithmetic  50.8 us (8%)
  starting transfers between devices  20.3 us (3%)
  between operations  14.2 us (2%)
    psum x2, waiting for transfers between devices, shards(): gram = lax.psum(local_gram(current, node_total), ('region', 'dom'))  241 us
    psum x1, waiting for transfers between devices, rayleigh_sum(): return lax.psum(partial_value, ('region', 'dom'))  125 us
    dot_general x18, matrix products, add_group(): jnp.einsum('rt,tiw->riw', select, products, precision=HIGH)  63.3 us
    gather x18, local copies, waits for them, and re-layouts, add_group(): gathered = extended[col_part]  42.1 us
    dot_general x18, matrix products, add_group(): lax.dot_general(tile_part, gathered, (((2,), (1,)), ((0,), (0,))), prefer...  32.4 us
    while x72, local copies, waits for them, and re-layouts  25.8 us
    another operation x6, other arithmetic, shards(): factor = jnp.linalg.cholesky(gram)  24.8 us
    another operation x4, other arithmetic, shards(): lax.linalg.triangular_solve(factor, identity, left_side=True, lower=True)  20.9 us
  transfers between devices with their start and end apart: 11, of which 5 were waited for; matrix products, arithmetic and copies ran while one was open for 1% of the time, Pallas kernels for 0%

commit v1 on v0

v1 whole, which is shorter than its diff:
```python
import functools
import math

import jax
import jax.numpy as jnp
from jax import lax
from jax.experimental import pallas as pl
from jax.experimental.pallas import tpu as pltpu
from jax.sharding import PartitionSpec as P

ITERS = 2
F32 = jnp.float32
BF16 = jnp.bfloat16
MESH = pl.DeviceIdType.MESH
VM = pl.BlockSpec(memory_space=pltpu.VMEM)
SM = pl.BlockSpec(memory_space=pltpu.SMEM)
LIMIT = 48 * 1024 * 1024


def reduce_kernel(regions, doms, pieces, x_ref, o_ref, scat, res, send_a, recv_a, send_b, recv_b):
    total = regions * doms
    stride = total // pieces
    me = lax.axis_index("dom") * regions + lax.axis_index("region")
    mine = me // stride
    owner = lax.rem(me, stride) == 0

    def device(flat):
        return (lax.rem(flat, regions), flat // regions)

    barrier = pltpu.get_barrier_semaphore()

    def greet(off, carry):
        pl.semaphore_signal(
            barrier, inc=1, device_id=device(lax.rem(me + off, total)), device_id_type=MESH
        )
        return carry

    lax.fori_loop(1, total, greet, 0)
    pl.semaphore_wait(barrier, total - 1)

    def scatter(step, carry):
        piece = lax.rem(mine + step, pieces)
        target = piece * stride

        @pl.when(target != me)
        def _():
            pltpu.make_async_remote_copy(
                src_ref=x_ref.at[piece],
                dst_ref=scat.at[lax.rem(me - target - 1 + total, total)],
                send_sem=send_a,
                recv_sem=recv_a,
                device_id=device(target),
                device_id_type=MESH,
            ).start()

        return carry

    lax.fori_loop(0, pieces, scatter, 0)

    @pl.when(owner)
    def _():
        pltpu.make_async_copy(scat, scat, recv_a).wait()
        parts = [scat[s] for s in range(total - 1)] + [x_ref[mine]]
        while len(parts) > 1:
            parts = [a + b for a, b in zip(parts[::2], parts[1::2])] + (
                [parts[-1]] if len(parts) % 2 else []
            )
        res[mine] = parts[0]

        def spread(off, carry):
            pltpu.make_async_remote_copy(
                src_ref=res.at[mine],
                dst_ref=res.at[mine],
                send_sem=send_b,
                recv_sem=recv_b,
                device_id=device(lax.rem(me + off, total)),
                device_id_type=MESH,
            ).start()
            return carry

        lax.fori_loop(1, total, spread, 0)
        rest = res.at[pl.ds(0, pieces - 1)]
        pltpu.make_async_copy(rest, rest, recv_b).wait()
        sent = x_ref.at[pl.ds(0, pieces - 1)]
        pltpu.make_async_copy(sent, sent, send_a).wait()
        pltpu.make_async_copy(scat, scat, send_b).wait()

    @pl.when(jnp.logical_not(owner))
    def _():
        pltpu.make_async_copy(res, res, recv_b).wait()
        pltpu.make_async_copy(x_ref, x_ref, send_a).wait()

    o_ref[...] = res[...]


def all_sum(x, regions, doms, ident):
    rows, lanes = x.shape
    total = regions * doms
    pieces = min(total, 16)
    shape = (pieces, rows // pieces, lanes)
    out = pl.pallas_call(
        functools.partial(reduce_kernel, regions, doms, pieces),
        out_shape=jax.ShapeDtypeStruct(shape, F32),
        in_specs=[VM],
        out_specs=VM,
        scratch_shapes=[
            pltpu.VMEM((total - 1,) + shape[1:], F32),
            pltpu.VMEM(shape, F32),
            pltpu.SemaphoreType.DMA,
            pltpu.SemaphoreType.DMA,
            pltpu.SemaphoreType.DMA,
            pltpu.SemaphoreType.DMA,
        ],
        compiler_params=pltpu.CompilerParams(collective_id=ident, has_side_effects=True),
        name="allsum" + str(ident),
    )(x.reshape(shape))
    return out.reshape(rows, lanes)


def invert_rows(gram, out_ref):
    size = gram.shape[0]
    tiles = [gram[8 * j : 8 * j + 8, :] for j in range(size // 8)]
    lane = lax.broadcasted_iota(jnp.int32, (8, size), 1)
    sub = lax.broadcasted_iota(jnp.int32, (8, size), 0)
    lane1 = lax.broadcasted_iota(jnp.int32, (1, size), 1)
    for k in range(size):
        kb, ks = divmod(k, 8)
        row = tiles[kb][ks : ks + 1, :]
        pivot = jnp.broadcast_to(row[:, k : k + 1], (1, size))
        row = jnp.where(lane1 == k, 1.0, row)
        root = lax.rsqrt(pivot)
        root = root * (1.5 - 0.5 * pivot * root * root)
        out_ref[k : k + 1, :] = jnp.where(lane1 <= k, row * root, 0.0)
        scaled = row * (root * root)
        here = lane == k
        for j in range(kb, size // 8):
            col = jnp.broadcast_to(tiles[j][:, k : k + 1], (8, size))
            if j == kb:
                if ks == 7:
                    continue
                live = sub > ks
                col = jnp.where(live, col, 0.0)
                base = jnp.where(here & live, 0.0, tiles[j])
            else:
                base = jnp.where(here, 0.0, tiles[j])
            tiles[j] = base - col * scaled


def ortho_kernel(gram_ref, cur_ref, list_ref, count_ref, basis_ref, p0, p1, p2, p3, inv):
    invert_rows(gram_ref[...], inv)
    full = inv[...]
    high = full.astype(BF16)
    low = (full - high.astype(F32)).astype(BF16)
    both = jnp.concatenate([high, low], axis=0)
    width = full.shape[0]

    def rotate(t, carry):
        prod = lax.dot_general(
            cur_ref[t], both, (((1,), (1,)), ((), ())), preferred_element_type=F32
        )
        basis_ref[t] = (prod[:, :width] + prod[:, width:]).astype(BF16)
        return carry

    lax.fori_loop(0, basis_ref.shape[0], rotate, 0, unroll=4)
    for d, out in enumerate((p0, p1, p2, p3)):
        for s in range(out.shape[0]):
            live = s < count_ref[0, d]

            @pl.when(live)
            def _():
                out[s] = basis_ref[list_ref[0, d, s]]

            @pl.when(jnp.logical_not(live))
            def _():
                out[s] = jnp.zeros(out.shape[1:], BF16)


def orthonormalize(gram, current, send_list, send_count):
    capacity = send_list.shape[2]
    tile = current.shape[1:]
    pack = jax.ShapeDtypeStruct((capacity,) + tile, BF16)
    return pl.pallas_call(
        ortho_kernel,
        out_shape=(jax.ShapeDtypeStruct(current.shape, BF16), pack, pack, pack, pack),
        in_specs=[VM, VM, SM, SM],
        out_specs=(VM,) * 5,
        scratch_shapes=[pltpu.VMEM(gram.shape, F32)],
        compiler_params=pltpu.CompilerParams(vmem_limit_bytes=LIMIT),
        name="ortho",
    )(gram, current, send_list, send_count)


def graph_kernel(
    scale_gram, scale_ray, row_ref, col_ref, tiles_ref, basis_ref, r0, r1, r2, r3,
    cur_ref, gram_ref, ray_ref, ext, acc,
):
    step = pl.program_id(0)
    group = tiles_ref.shape[0]
    row_tiles = basis_ref.shape[0]
    capacity = r0.shape[0]

    @pl.when(step == 0)
    def _():
        ext[0:row_tiles] = basis_ref[...]
        for d, r in enumerate((r0, r1, r2, r3)):
            first = row_tiles + d * capacity
            ext[first : first + capacity] = r[...]
        acc[...] = jnp.zeros_like(acc)

    for t in range(group):
        row = row_ref[step * group + t]
        col = col_ref[step * group + t]
        acc[row] += jnp.dot(tiles_ref[t], ext[col], preferred_element_type=F32)

    @pl.when(step == pl.num_programs(0) - 1)
    def _():
        width = gram_ref.shape[0]

        def fold(t, total):
            applied = acc[t]
            high = applied.astype(BF16)
            low = (applied - high.astype(F32)).astype(BF16)
            cur_ref[t] = high
            left = jnp.concatenate([basis_ref[t], high], axis=1)
            right = jnp.concatenate([high, low], axis=1)
            return total + lax.dot_general(
                left, right, (((0,), (0,)), ((), ())), preferred_element_type=F32
            )

        total = lax.fori_loop(
            0, row_tiles, fold, jnp.zeros((2 * width, 2 * width), F32), unroll=2
        )
        ray_ref[...] = (total[:width, :width] + total[:width, width:]) * scale_ray
        gram_ref[...] = total[width:, :width] * scale_gram


def graph(basis, received, tiles, tile_row, tile_col, node_total):
    row_tiles = basis.shape[0]
    tile = basis.shape[1:]
    stored = tiles.shape[0]
    group = next(g for g in (36, 32, 24, 16, 8, 4, 2, 1) if stored % g == 0)
    capacity = received[0].shape[0]

    def fixed(shape):
        return pl.BlockSpec(shape, lambda i: (0,) * len(shape))

    width = tile[1]
    return pl.pallas_call(
        functools.partial(graph_kernel, 1.0 / node_total, 1.0 / math.sqrt(node_total)),
        grid=(stored // group,),
        out_shape=(
            jax.ShapeDtypeStruct(basis.shape, BF16),
            jax.ShapeDtypeStruct((width, width), F32),
            jax.ShapeDtypeStruct((width, width), F32),
        ),
        in_specs=[SM, SM, pl.BlockSpec((group,) + tiles.shape[1:], lambda i: (i, 0, 0)), fixed(basis.shape)]
        + [fixed(received[0].shape)] * 4,
        out_specs=(fixed(basis.shape), fixed((width, width)), fixed((width, width))),
        scratch_shapes=[
            pltpu.VMEM((row_tiles + 4 * capacity,) + tile, BF16),
            pltpu.VMEM((row_tiles,) + tile, F32),
        ],
        compiler_params=pltpu.CompilerParams(vmem_limit_bytes=LIMIT),
        name="graph",
    )(tile_row, tile_col, tiles, basis, *received)


def exchange(packed):
    received = []
    for axis, down, up in (("dom", packed[0], packed[1]), ("region", packed[2], packed[3])):
        count = lax.axis_size(axis)
        forward = [(i, i + 1) for i in range(count - 1)]
        backward = [(i + 1, i) for i in range(count - 1)]
        received.append(lax.ppermute(down, axis, forward))
        received.append(lax.ppermute(up, axis, backward))
    return received


def shards(x_init, tiles, tile_row, tile_col, send_list, send_count):
    row_count, vectors = x_init.shape
    tile_size = tiles.shape[1]
    row_tiles = row_count // tile_size
    regions, doms = lax.axis_size("region"), lax.axis_size("dom")
    node_total = row_count * regions * doms
    part = lax.dot_general(
        x_init, x_init, (((0,), (0,)), ((), ())), preferred_element_type=F32
    ) * (1.0 / node_total)
    current = x_init.reshape(row_tiles, tile_size, vectors)
    rays = []
    for iteration in range(ITERS):
        gram = all_sum(part, regions, doms, iteration)
        basis, *packed = orthonormalize(gram, current, send_list, send_count)
        received = exchange(packed)
        current, part, ray = graph(basis, received, tiles, tile_row, tile_col, node_total)
        rays.append(ray)
    ritz = all_sum(jnp.concatenate(rays, axis=0), regions, doms, ITERS)
    return basis.reshape(row_count, vectors), ritz.reshape(ITERS, vectors, vectors)


def solution(mesh):
    both = ("region", "dom")
    in_specs = (
        P(both, None),
        P(both, None, None),
        P(both),
        P(both),
        P(both, None, None),
        P(both, None),
    )
    return jax.shard_map(
        shards, mesh=mesh, in_specs=in_specs, out_specs=(P(both, None), P()), check_vma=False
    )
```

time: 655 us -> 150 us (0.23)
  waiting for transfers between devices: 376 us -> 14.1 us
  Pallas kernels: 0 us -> 106 us
  matrix products: 108 us -> 2.67 us
  local copies, waits for them, and re-layouts: 83.8 us -> 9.02 us
  other arithmetic: 50.8 us -> 0.66 us
  between operations: 14.2 us -> 0.85 us
    psum x3 -> x0, waiting for transfers between devices: 366 us -> none  [the longest x2 241 us: shards(): gram = lax.psum(local_gram(current, node_total), ('region', 'dom'))]
    pallas_call x0 -> x7, Pallas kernels: none -> 106 us  [the longest x3 49.9 us: all_sum(): pl.pallas_call(functools.partial(reduce_kernel, regions, doms, pieces), o...]
    dot_general x42 -> x1, matrix products: 108 us -> 2.67 us  [shards(): lax.dot_general(x_init, x_init, (((0,), (0,)), ((), ())), preferred_eleme...]
    another operation x11 -> x0, other arithmetic: 47.2 us -> none  [the longest x6 24.8 us: shards(): factor = jnp.linalg.cholesky(gram)]
    gather x20 -> x0, local copies, waits for them, and re-layouts: 44.5 us -> none  [the longest x18 42.1 us: add_group(): gathered = extended[col_part]]
    while x74 -> x0, local copies, waits for them, and re-layouts: 31.2 us -> none
  transfers between devices with their start and end apart: 11 -> 8, of which waited for: 5 -> 2; matrix products, arithmetic and copies ran while one was open for 1% -> 0% of each run, Pallas kernels for 0% -> 0%
where the time goes in v1:
time: 150 us; the launch traced here: 149 us
  Pallas kernels  106 us (71%)
  starting transfers between devices  14.8 us (10%)
  waiting for transfers between devices  14.1 us (9%)
  local copies, waits for them, and re-layouts  9.02 us (6%)
  matrix products  2.67 us (2%)
    pallas_call x3, Pallas kernels, all_sum(): pl.pallas_call(functools.partial(reduce_kernel, regions, doms, pieces), o...  49.9 us
    pallas_call x2, Pallas kernels, orthonormalize(): pl.pallas_call(ortho_kernel, out_shape=(jax.ShapeDtypeStruct(current.shap...  30.6 us
    pallas_call x2, Pallas kernels, graph(): pl.pallas_call(functools.partial(graph_kernel, 1.0 / node_total, 1.0 / ma...  25.9 us
    ppermute x4, waiting for transfers between devices, exchange(): received.append(lax.ppermute(down, axis, forward))  14.1 us
    ppermute x4, starting transfers between devices, exchange(): received.append(lax.ppermute(down, axis, forward))  9.67 us
    unnamed x27, local copies, waits for them, and re-layouts  9.02 us
    ppermute x4, starting transfers between devices, exchange(): received.append(lax.ppermute(up, axis, backward))  5.17 us
  transfers between devices with their start and end apart: 8, of which 2 were waited for; matrix products, arithmetic and copies ran while one was open for 0% of the time, Pallas kernels for 0%

profile of v1, /device:TPU:0, one launch (start us, length us, event | category | flops | bytes accessed | tf_op | source)
XLA Modules:
  0.0 148.7 jit_solution(8973460785631442882)
XLA Ops:
  0.7 0.0 copy-start.10
  0.7 0.0 copy-start.8
  0.7 2.7 %fusion.x_ref = f32[16,8,128]{2,1,0:T(8,128)} fusion(bf16[4096,128]{1,0:T(8,128)(2,1)} %param.6), kind=kOutput, calls=%fused_computation.1 | convolution fusion | flops 134234112 | bytes 1114112 | tf_op jit(solution)/shard_map/dot_general | solution.py:285
  3.3 17.7 %allsum0.1 = f32[16,8,128]{2,1,0:T(8,128)} custom-call(f32[16,8,128]{2,1,0:T(8,128)} %fusion.x_ref), custom_call_target="tpu_custom_call" | custom-call | tf_op jit(solution)/shard_map/allsum0/pallas_call | solution.py:101
  21.1 1.2 copy-done
  22.3 0.8 copy-done.3
  23.1 0.7 copy-done.5
  23.8 0.7 copy-done.11
  24.5 14.8 %ortho.2 = (bf16[32,128,128]{2,1,0:T(8,128)(2,1)S(1)}, bf16[8,128,128]{2,1,0:T(8,128)(2,1)S(1)}, bf16[8,128,128]{2,1,0:T(8,128)(2,1)S(1)}, bf16[8,128,128]{2,1,0:T(8,128)(2,1)S(1)}, bf16[8,128,128]{2,1,0:T(8,128)(2,1)S(1)}) custom-call(f32[128,128]{1,0:T(8,128)S(1)} %bitcast.14, bf16[32,128,128]{2,1,0:T(8,128)(2,1)S(1)} %bitcast.11, ...), custom_call_target="tpu_custom_call" | custom-call | tf_op jit(solution)/shard_map/ortho/pallas_call | solution.py:182
  39.3 2.7 %collective-permute-start = (bf16[8,128,128]{2,1,0:T(8,128)(2,1)S(1)}, bf16[8,128,128]{2,1,0:T(8,128)(2,1)S(1)}, u32[]{:S(2)}, u32[]{:S(2)}) collective-permute-start(bf16[8,128,128]{2,1,0:T(8,128)(2,1)S(1)} %get-tuple-element.17), channel_id=1, source_target_pairs={{0,1},{1,2},{2,3},{3,4},{4,5},{5,6},{6,7},{8,9},{9,10},{10,11},{11... | collective-permute-start | bytes 786440 | tf_op jit(solution)/shard_map/ppermute | solution.py:274
  42.0 1.3 collective-permute-start.1
  43.3 1.8 %collective-permute-start.2 = (bf16[8,128,128]{2,1,0:T(8,128)(2,1)S(1)}, bf16[8,128,128]{2,1,0:T(8,128)(2,1)S(1)}, u32[]{:S(2)}, u32[]{:S(2)}) collective-permute-start(bf16[8,128,128]{2,1,0:T(8,128)(2,1)S(1)} %get-tuple-element.19), channel_id=1, source_target_pairs={{0,8},{8,16},{16,24},{1,9},{9,17},{17,25},{2,10},{10,18},{18,26},{... | collective-permute-start | bytes 786440 | tf_op jit(solution)/shard_map/ppermute | solution.py:274
  45.1 1.3 collective-permute-start.3
  46.4 7.1 %collective-permute-done.r0 = bf16[8,128,128]{2,1,0:T(8,128)(2,1)S(1)} collective-permute-done((bf16[8,128,128]{2,1,0:T(8,128)(2,1)S(1)}, bf16[8,128,128]{2,1,0:T(8,128)(2,1)S(1)}, u32[]{:S(2)}, u32[]{:S(2)}) %collective-permute-start) | collective-permute-done | bytes 262176 | tf_op jit(solution)/shard_map/ppermute | solution.py:274
  53.5 0.7 copy-done.7
  54.1 0.7 copy-done.9
  54.8 12.4 %graph.2 = (bf16[32,128,128]{2,1,0:T(8,128)(2,1)S(1)}, f32[128,128]{1,0:T(8,128)S(1)}, f32[128,128]{1,0:T(8,128)S(1)}) custom-call(s32[288]{0:T(512)S(1)} %copy-done.7, s32[288]{0:T(512)S(1)} %copy-done.9, bf16[288,128,128]{2,1,0:T(8,128)(2,1)} %tiles_ref.3, bf16[32,128,128]{2,1,0:T(8,128)(2,1)S(1)} %get-tuple-element.16.basis_ref, ...), custom_call_target="tpu_custom_call" | custom-call | tf_op jit(solution)/shard_map/graph/pallas_call | solution.py:248
  67.3 0.6 copy-done.4
  67.9 15.1 %allsum1.1 = f32[16,8,128]{2,1,0:T(8,128)} custom-call(f32[16,8,128]{2,1,0:T(8,128)} %bitcast.15), custom_call_target="tpu_custom_call" | custom-call | tf_op jit(solution)/shard_map/allsum1/pallas_call | solution.py:101
  83.0 0.8 copy-done.2
  83.8 15.8 %ortho.3 = (bf16[32,128,128]{2,1,0:T(8,128)(2,1)}, bf16[8,128,128]{2,1,0:T(8,128)(2,1)S(1)}, bf16[8,128,128]{2,1,0:T(8,128)(2,1)S(1)}, bf16[8,128,128]{2,1,0:T(8,128)(2,1)S(1)}, bf16[8,128,128]{2,1,0:T(8,128)(2,1)S(1)}) custom-call(f32[128,128]{1,0:T(8,128)S(1)} %bitcast.13, bf16[32,128,128]{2,1,0:T(8,128)(2,1)S(1)} %get-tuple-element.22.cur_ref, ...), custom_call_target="tpu_custom_call" | custom-call | tf_op jit(solution)/shard_map/ortho/pallas_call | solution.py:182
  99.6 3.6 %collective-permute-start.4 = (bf16[8,128,128]{2,1,0:T(8,128)(2,1)S(1)}, bf16[8,128,128]{2,1,0:T(8,128)(2,1)S(1)}, u32[]{:S(2)}, u32[]{:S(2)}) collective-permute-start(bf16[8,128,128]{2,1,0:T(8,128)(2,1)S(1)} %get-tuple-element.25), channel_id=1, source_target_pairs={{0,1},{1,2},{2,3},{3,4},{4,5},{5,6},{6,7},{8,9},{9,10},{10,11},{11... | collective-permute-start | bytes 786440 | tf_op jit(solution)/shard_map/ppermute | solution.py:274
  103.2 1.3 collective-permute-start.5
  104.5 1.7 %collective-permute-start.6 = (bf16[8,128,128]{2,1,0:T(8,128)(2,1)S(1)}, bf16[8,128,128]{2,1,0:T(8,128)(2,1)S(1)}, u32[]{:S(2)}, u32[]{:S(2)}) collective-permute-start(bf16[8,128,128]{2,1,0:T(8,128)(2,1)S(1)} %get-tuple-element.27), channel_id=1, source_target_pairs={{0,8},{8,16},{16,24},{1,9},{9,17},{17,25},{2,10},{10,18},{18,26},{... | collective-permute-start | bytes 786440 | tf_op jit(solution)/shard_map/ppermute | solution.py:274
  106.2 1.3 collective-permute-start.7
  107.5 7.1 %collective-permute-done.4.r0 = bf16[8,128,128]{2,1,0:T(8,128)(2,1)S(1)} collective-permute-done((bf16[8,128,128]{2,1,0:T(8,128)(2,1)S(1)}, bf16[8,128,128]{2,1,0:T(8,128)(2,1)S(1)}, u32[]{:S(2)}, u32[]{:S(2)}) %collective-permute-start.4) | collective-permute-done | bytes 262176 | tf_op jit(solution)/shard_map/ppermute | solution.py:274
  114.5 0.0 copy-start.1
  114.6 1.2 copy-done.1
  115.8 13.5 %graph.3 = (bf16[32,128,128]{2,1,0:T(8,128)(2,1)}, f32[128,128]{1,0:T(8,128)}, f32[128,128]{1,0:T(8,128)S(1)}) custom-call(s32[288]{0:T(512)S(1)} %copy-done.8, s32[288]{0:T(512)S(1)} %copy-done.10, bf16[288,128,128]{2,1,0:T(8,128)(2,1)} %tiles_ref.3, bf16[32,128,128]{2,1,0:T(8,128)(2,1)S(1)} %copy-done.1, ...), custom_call_target="tpu_custom_call" | custom-call | tf_op jit(solution)/shard_map/graph/pallas_call | solution.py:248
  129.2 0.7 pad_maximum_fusion
  129.9 17.2 %allsum2.1 = f32[16,16,128]{2,1,0:T(8,128)} custom-call(f32[16,16,128]{2,1,0:T(8,128)} %bitcast.16), custom_call_target="tpu_custom_call" | custom-call | tf_op jit(solution)/shard_map/allsum2/pallas_call | solution.py:101
  147.1 1.6 %copy.9 = f32[2,128,128]{2,1,0:T(8,128)} copy(f32[2,128,128]{2,1,0:T(8,128)} %bitcast.17) | data formatting | bytes 262144
  (20 shorter events, 0.1 us)
Async XLA Ops:
  0.6 82.3 %copy-start.12 = (s32[1,4]{1,0:T(1,128)S(1)}, s32[1,4]{1,0:T(1,128)}, u32[]{:S(2)}) copy-start(s32[1,4]{1,0:T(1,128)} %count_ref.3) | copy-start | bytes 52
  0.6 82.3 %copy-start.6 = (s32[1,4,8]{2,1,0:T(4,128)S(1)}, s32[1,4,8]{2,1,0:T(4,128)}, u32[]{:S(2)}) copy-start(s32[1,4,8]{2,1,0:T(4,128)} %list_ref.3) | copy-start | bytes 388
  0.7 113.9 %copy-start.10 = (s32[288]{0:T(512)S(1)}, s32[288]{0:T(512)}, u32[]{:S(2)}) copy-start(s32[288]{0:T(512)} %col_ref.3) | copy-start | bytes 3460
  0.7 113.9 %copy-start.8 = (s32[288]{0:T(512)S(1)}, s32[288]{0:T(512)}, u32[]{:S(2)}) copy-start(s32[288]{0:T(512)} %row_ref.3) | copy-start | bytes 3460
  21.1 1.2 copy-start
  22.3 0.8 copy-start.3
  23.1 0.7 copy-start.5
  23.8 0.7 copy-start.11
  39.3 14.1 %collective-permute-start = (bf16[8,128,128]{2,1,0:T(8,128)(2,1)S(1)}, bf16[8,128,128]{2,1,0:T(8,128)(2,1)S(1)}, u32[]{:S(2)}, u32[]{:S(2)}) collective-permute-start(bf16[8,128,128]{2,1,0:T(8,128)(2,1)S(1)} %get-tuple-element.17), channel_id=1, source_target_pairs={{0,1},{1,2},{2,3},{3,4},{4,5},{5,6},{6,7},{8,9},{9,10},{10,11},{11... | collective-permute-start | bytes 786440 | tf_op jit(solution)/shard_map/ppermute | solution.py:274
  42.0 11.4 %collective-permute-start.1 = (bf16[8,128,128]{2,1,0:T(8,128)(2,1)S(1)}, bf16[8,128,128]{2,1,0:T(8,128)(2,1)S(1)}, u32[]{:S(2)}, u32[]{:S(2)}) collective-permute-start(bf16[8,128,128]{2,1,0:T(8,128)(2,1)S(1)} %get-tuple-element.18), channel_id=1, source_target_pairs={{1,0},{2,1},{3,2},{4,3},{5,4},{6,5},{7,6},{9,8},{10,9},{11,10},{12... | collective-permute-start | bytes 786440 | tf_op jit(solution)/shard_map/ppermute | solution.py:275
  43.3 10.1 %collective-permute-start.2 = (bf16[8,128,128]{2,1,0:T(8,128)(2,1)S(1)}, bf16[8,128,128]{2,1,0:T(8,128)(2,1)S(1)}, u32[]{:S(2)}, u32[]{:S(2)}) collective-permute-start(bf16[8,128,128]{2,1,0:T(8,128)(2,1)S(1)} %get-tuple-element.19), channel_id=1, source_target_pairs={{0,8},{8,16},{16,24},{1,9},{9,17},{17,25},{2,10},{10,18},{18,26},{... | collective-permute-start | bytes 786440 | tf_op jit(solution)/shard_map/ppermute | solution.py:274
  45.1 8.4 %collective-permute-start.3 = (bf16[8,128,128]{2,1,0:T(8,128)(2,1)S(1)}, bf16[8,128,128]{2,1,0:T(8,128)(2,1)S(1)}, u32[]{:S(2)}, u32[]{:S(2)}) collective-permute-start(bf16[8,128,128]{2,1,0:T(8,128)(2,1)S(1)} %get-tuple-element.20), channel_id=1, source_target_pairs={{8,0},{16,8},{24,16},{9,1},{17,9},{25,17},{10,2},{18,10},{26,18},{... | collective-permute-start | bytes 786440 | tf_op jit(solution)/shard_map/ppermute | solution.py:275
  53.4 0.7 copy-start.7
  54.1 0.7 copy-start.9
  67.3 0.6 copy-start.4
  83.0 0.8 copy-start.2
  99.6 14.9 %collective-permute-start.4 = (bf16[8,128,128]{2,1,0:T(8,128)(2,1)S(1)}, bf16[8,128,128]{2,1,0:T(8,128)(2,1)S(1)}, u32[]{:S(2)}, u32[]{:S(2)}) collective-permute-start(bf16[8,128,128]{2,1,0:T(8,128)(2,1)S(1)} %get-tuple-element.25), channel_id=1, source_target_pairs={{0,1},{1,2},{2,3},{3,4},{4,5},{5,6},{6,7},{8,9},{9,10},{10,11},{11... | collective-permute-start | bytes 786440 | tf_op jit(solution)/shard_map/ppermute | solution.py:274
  103.2 11.4 %collective-permute-start.5 = (bf16[8,128,128]{2,1,0:T(8,128)(2,1)S(1)}, bf16[8,128,128]{2,1,0:T(8,128)(2,1)S(1)}, u32[]{:S(2)}, u32[]{:S(2)}) collective-permute-start(bf16[8,128,128]{2,1,0:T(8,128)(2,1)S(1)} %get-tuple-element.26), channel_id=1, source_target_pairs={{1,0},{2,1},{3,2},{4,3},{5,4},{6,5},{7,6},{9,8},{10,9},{11,10},{12... | collective-permute-start | bytes 786440 | tf_op jit(solution)/shard_map/ppermute | solution.py:275
  104.5 10.1 %collective-permute-start.6 = (bf16[8,128,128]{2,1,0:T(8,128)(2,1)S(1)}, bf16[8,128,128]{2,1,0:T(8,128)(2,1)S(1)}, u32[]{:S(2)}, u32[]{:S(2)}) collective-permute-start(bf16[8,128,128]{2,1,0:T(8,128)(2,1)S(1)} %get-tuple-element.27), channel_id=1, source_target_pairs={{0,8},{8,16},{16,24},{1,9},{9,17},{17,25},{2,10},{10,18},{18,26},{... | collective-permute-start | bytes 786440 | tf_op jit(solution)/shard_map/ppermute | solution.py:274
  106.2 8.4 %collective-permute-start.7 = (bf16[8,128,128]{2,1,0:T(8,128)(2,1)S(1)}, bf16[8,128,128]{2,1,0:T(8,128)(2,1)S(1)}, u32[]{:S(2)}, u32[]{:S(2)}) collective-permute-start(bf16[8,128,128]{2,1,0:T(8,128)(2,1)S(1)} %get-tuple-element.28), channel_id=1, source_target_pairs={{8,0},{16,8},{24,16},{9,1},{17,9},{25,17},{10,2},{18,10},{26,18},{... | collective-permute-start | bytes 786440 | tf_op jit(solution)/shard_map/ppermute | solution.py:275
  114.5 1.2 copy-start.1

commit v2 on v1

v2 whole, which is shorter than its diff:
```python
import functools
import math

import jax
import jax.numpy as jnp
from jax import lax
from jax.experimental import pallas as pl
from jax.experimental.pallas import tpu as pltpu
from jax.sharding import PartitionSpec as P

ITERS = 2
F32 = jnp.float32
BF16 = jnp.bfloat16
MESH = pl.DeviceIdType.MESH
VM = pl.BlockSpec(memory_space=pltpu.VMEM)
SM = pl.BlockSpec(memory_space=pltpu.SMEM)
LIMIT = 48 * 1024 * 1024


def reduce_kernel(regions, doms, pieces, x_ref, o_ref, scat, res, send_a, recv_a, send_b, recv_b):
    total = regions * doms
    stride = total // pieces
    me = lax.axis_index("dom") * regions + lax.axis_index("region")
    mine = me // stride
    owner = lax.rem(me, stride) == 0

    def away(off):
        flat = me + off
        flat = jnp.where(flat >= total, flat - total, flat)
        return (lax.rem(flat, regions), flat // regions)

    barrier = pltpu.get_barrier_semaphore()

    def greet(off, carry):
        pl.semaphore_signal(
            barrier, inc=1, device_id=away(off), device_id_type=MESH
        )
        return carry

    lax.fori_loop(1, total, greet, 0)
    pl.semaphore_wait(barrier, total - 1)

    def scatter(step, carry):
        piece = lax.rem(mine + step, pieces)
        target = piece * stride

        @pl.when(target != me)
        def _():
            pltpu.make_async_remote_copy(
                src_ref=x_ref.at[piece],
                dst_ref=scat.at[lax.rem(me - target - 1 + total, total)],
                send_sem=send_a,
                recv_sem=recv_a,
                device_id=(lax.rem(target, regions), target // regions),
                device_id_type=MESH,
            ).start()

        return carry

    lax.fori_loop(0, pieces, scatter, 0)

    @pl.when(owner)
    def _():
        pltpu.make_async_copy(scat, scat, recv_a).wait()
        parts = [scat[s] for s in range(total - 1)] + [x_ref[mine]]
        while len(parts) > 1:
            parts = [a + b for a, b in zip(parts[::2], parts[1::2])] + (
                [parts[-1]] if len(parts) % 2 else []
            )
        res[mine] = parts[0]

        def spread(off, carry):
            pltpu.make_async_remote_copy(
                src_ref=res.at[mine],
                dst_ref=res.at[mine],
                send_sem=send_b,
                recv_sem=recv_b,
                device_id=away(off),
                device_id_type=MESH,
            ).start()
            return carry

        lax.fori_loop(1, total, spread, 0)
        rest = res.at[pl.ds(0, pieces - 1)]
        pltpu.make_async_copy(rest, rest, recv_b).wait()
        sent = x_ref.at[pl.ds(0, pieces - 1)]
        pltpu.make_async_copy(sent, sent, send_a).wait()
        pltpu.make_async_copy(scat, scat, send_b).wait()

    @pl.when(jnp.logical_not(owner))
    def _():
        pltpu.make_async_copy(res, res, recv_b).wait()
        pltpu.make_async_copy(x_ref, x_ref, send_a).wait()

    o_ref[...] = res[...]


def all_sum(x, regions, doms, ident):
    rows, lanes = x.shape
    total = regions * doms
    pieces = min(total, 16)
    shape = (pieces, rows // pieces, lanes)
    out = pl.pallas_call(
        functools.partial(reduce_kernel, regions, doms, pieces),
        out_shape=jax.ShapeDtypeStruct(shape, F32),
        in_specs=[VM],
        out_specs=VM,
        scratch_shapes=[
            pltpu.VMEM((total - 1,) + shape[1:], F32),
            pltpu.VMEM(shape, F32),
            pltpu.SemaphoreType.DMA,
            pltpu.SemaphoreType.DMA,
            pltpu.SemaphoreType.DMA,
            pltpu.SemaphoreType.DMA,
        ],
        compiler_params=pltpu.CompilerParams(collective_id=ident, has_side_effects=True),
        name="allsum" + str(ident),
    )(x.reshape(shape))
    return out.reshape(rows, lanes)


def invert_rows(gram, out_ref):
    size = gram.shape[0]
    count = size // 8
    tiles = [gram[8 * j : 8 * j + 8, :] for j in range(count)]
    lane = lax.broadcasted_iota(jnp.int32, (8, size), 1)
    sub = lax.broadcasted_iota(jnp.int32, (8, size), 0)

    def row(tile, c):
        return jnp.broadcast_to(tile[c : c + 1, :], (8, size))

    def column(tile, c):
        return jnp.broadcast_to(tile[:, c : c + 1], (8, size))

    for kb in range(count):
        first = 8 * kb
        inside = (lane >= first) & (lane < first + 8)
        cols = [column(tiles[kb], first + c) for c in range(8)]
        rows = jnp.where(inside, jnp.where(lane == sub + first, 1.0, 0.0), tiles[kb])
        roots = jnp.zeros((8, size), F32)
        lower, scaled = [], []
        for c in range(8):
            pivot = row(cols[c], c)
            root = lax.rsqrt(pivot)
            root = root * (1.5 - 0.5 * pivot * root * root)
            roots = jnp.where(sub == c, root, roots)
            ratio = cols[c] * (root * root)
            mine = row(rows, c)
            scaled.append(mine * (root * root))
            lower.append(ratio)
            if c < 7:
                rows = rows - jnp.where(sub > c, ratio, 0.0) * mine
                for later in range(c + 1, 8):
                    cols[later] = cols[later] - ratio * row(cols[c], later)
        out_ref[first : first + 8, :] = jnp.where(lane <= sub + first, rows * roots, 0.0)
        for i in range(7, 0, -1):
            for c in range(i):
                scaled[c] = scaled[c] - row(lower[c], i) * scaled[i]
        for j in range(kb + 1, count):
            terms = [column(tiles[j], first + c) * scaled[c] for c in range(8)]
            while len(terms) > 1:
                terms = [p + q for p, q in zip(terms[::2], terms[1::2])]
            tiles[j] = jnp.where(inside, 0.0, tiles[j]) - terms[0]


def invert_kernel(gram_ref, both_ref, inv):
    width = gram_ref.shape[0]
    invert_rows(gram_ref[...], inv)
    full = inv[...]
    high = full.astype(BF16)
    both_ref[0:width] = high
    both_ref[width : 2 * width] = (full - high.astype(F32)).astype(BF16)


def inverse_factor(gram):
    width = gram.shape[0]
    return pl.pallas_call(
        invert_kernel,
        out_shape=jax.ShapeDtypeStruct((2 * width, width), BF16),
        in_specs=[VM],
        out_specs=VM,
        scratch_shapes=[pltpu.VMEM(gram.shape, F32)],
        name="invert",
    )(gram)


def halo_kernel(regions, doms, both_ref, cur_ref, list_ref, ext_ref, own, send, send_sem, recv_sem):
    region, dom = lax.axis_index("region"), lax.axis_index("dom")
    capacity = send.shape[1]
    row_tiles = cur_ref.shape[0]
    width = cur_ref.shape[2]
    ways = (
        ((region, dom + 1), dom < doms - 1, dom > 0),
        ((region, dom - 1), dom > 0, dom < doms - 1),
        ((region + 1, dom), region < regions - 1, region > 0),
        ((region - 1, dom), region > 0, region < regions - 1),
    )
    barrier = pltpu.get_barrier_semaphore()
    for target, there, _ in ways:

        @pl.when(there)
        def _():
            pl.semaphore_signal(barrier, inc=1, device_id=target, device_id_type=MESH)

    both = both_ref[...]

    def rotate(t, carry):
        prod = lax.dot_general(
            cur_ref[t], both, (((1,), (1,)), ((), ())), preferred_element_type=F32
        )
        basis = (prod[:, :width] + prod[:, width:]).astype(BF16)
        ext_ref[t] = basis
        own[t] = basis
        return carry

    lax.fori_loop(0, row_tiles, rotate, 0, unroll=4)
    pl.semaphore_wait(barrier, sum(there.astype(jnp.int32) for _, there, _ in ways))

    def copy(d):
        return pltpu.make_async_remote_copy(
            src_ref=send.at[d],
            dst_ref=ext_ref.at[pl.ds(row_tiles + d * capacity, capacity)],
            send_sem=send_sem.at[d],
            recv_sem=recv_sem.at[d],
            device_id=ways[d][0],
            device_id_type=MESH,
        )

    for d in range(4):

        def pick(s, carry):
            send[d, s] = own[list_ref[0, d, s]]
            return carry

        lax.fori_loop(0, capacity, pick, 0, unroll=True)

    for d in range(4):

        @pl.when(ways[d][1])
        def _():
            copy(d).start()

    for d in range(4):

        @pl.when(ways[d][1])
        def _():
            copy(d).wait_send()

        @pl.when(ways[d][2])
        def _():
            copy(d).wait_recv()


def exchange(both, current, send_list, regions, doms, ident):
    capacity = send_list.shape[2]
    row_tiles = current.shape[0]
    tile = current.shape[1:]
    return pl.pallas_call(
        functools.partial(halo_kernel, regions, doms),
        out_shape=jax.ShapeDtypeStruct((row_tiles + 4 * capacity,) + tile, BF16),
        in_specs=[VM, VM, SM],
        out_specs=VM,
        scratch_shapes=[
            pltpu.VMEM(current.shape, BF16),
            pltpu.VMEM((4, capacity) + tile, BF16),
            pltpu.SemaphoreType.DMA((4,)),
            pltpu.SemaphoreType.DMA((4,)),
        ],
        compiler_params=pltpu.CompilerParams(
            collective_id=ident, has_side_effects=True, vmem_limit_bytes=LIMIT
        ),
        name="halo" + str(ident),
    )(both, current, send_list)


def graph_kernel(
    scale_gram, scale_ray, last, row_ref, col_ref, tiles_ref, ext, cur_ref, gram_ref, ray_ref, acc,
):
    step = pl.program_id(0)
    group = tiles_ref.shape[0]
    row_tiles = acc.shape[0]

    @pl.when(step == 0)
    def _():
        acc[...] = jnp.zeros_like(acc)

    for t in range(group):
        row = row_ref[step * group + t]
        col = col_ref[step * group + t]
        acc[row] += jnp.dot(tiles_ref[t], ext[col], preferred_element_type=F32)

    @pl.when(step == pl.num_programs(0) - 1)
    def _():
        width = gram_ref.shape[0]

        def fold(t, total):
            applied = acc[t]
            high = applied.astype(BF16)
            low = (applied - high.astype(F32)).astype(BF16)
            cur_ref[t] = ext[t] if last else high
            left = jnp.concatenate([ext[t], high], axis=1)
            right = jnp.concatenate([high, low], axis=1)
            return total + lax.dot_general(
                left, right, (((0,), (0,)), ((), ())), preferred_element_type=F32
            )

        total = lax.fori_loop(
            0, row_tiles, fold, jnp.zeros((2 * width, 2 * width), F32), unroll=2
        )
        ray_ref[...] = (total[:width, :width] + total[:width, width:]) * scale_ray
        gram_ref[...] = total[width:, :width] * scale_gram


def graph(ext, tiles, tile_row, tile_col, row_tiles, node_total, last):
    tile = ext.shape[1:]
    stored = tiles.shape[0]
    group = next(g for g in (36, 32, 24, 16, 8, 4, 2, 1) if stored % g == 0)
    width = tile[1]

    def fixed(shape):
        return pl.BlockSpec(shape, lambda i: (0,) * len(shape))

    own = (row_tiles,) + tile
    return pl.pallas_call(
        functools.partial(graph_kernel, 1.0 / node_total, 1.0 / math.sqrt(node_total), last),
        grid=(stored // group,),
        out_shape=(
            jax.ShapeDtypeStruct(own, BF16),
            jax.ShapeDtypeStruct((width, width), F32),
            jax.ShapeDtypeStruct((width, width), F32),
        ),
        in_specs=[
            SM,
            SM,
            pl.BlockSpec((group,) + tiles.shape[1:], lambda i: (i, 0, 0)),
            fixed(ext.shape),
        ],
        out_specs=(fixed(own), fixed((width, width)), fixed((width, width))),
        scratch_shapes=[pltpu.VMEM(own, F32)],
        compiler_params=pltpu.CompilerParams(vmem_limit_bytes=LIMIT),
        name="graph",
    )(tile_row, tile_col, tiles, ext)


def shards(x_init, tiles, tile_row, tile_col, send_list, send_count):
    row_count, vectors = x_init.shape
    tile_size = tiles.shape[1]
    row_tiles = row_count // tile_size
    regions, doms = lax.axis_size("region"), lax.axis_size("dom")
    node_total = row_count * regions * doms
    part = lax.dot_general(
        x_init, x_init, (((0,), (0,)), ((), ())), preferred_element_type=F32
    ) * (1.0 / node_total)
    current = x_init.reshape(row_tiles, tile_size, vectors)
    rays = []
    for iteration in range(ITERS):
        gram = all_sum(part, regions, doms, iteration)
        both = inverse_factor(gram)
        ext = exchange(both, current, send_list, regions, doms, ITERS + 1 + iteration)
        current, part, ray = graph(
            ext, tiles, tile_row, tile_col, row_tiles, node_total, iteration == ITERS - 1
        )
        rays.append(ray)
    ritz = all_sum(jnp.concatenate(rays, axis=0), regions, doms, ITERS)
    return current.reshape(row_count, vectors), ritz.reshape(ITERS, vectors, vectors)


def solution(mesh):
    both = ("region", "dom")
    in_specs = (
        P(both, None),
        P(both, None, None),
        P(both),
        P(both),
        P(both, None, None),
        P(both, None),
    )
    return jax.shard_map(
        shards, mesh=mesh, in_specs=in_specs, out_specs=(P(both, None), P()), check_vma=False
    )
```

time: 150 us -> 128 us (0.85)
  starting transfers between devices: 14.8 us -> 0 us
  waiting for transfers between devices: 14.1 us -> 0 us
  Pallas kernels: 106 us -> 119 us
  local copies, waits for them, and re-layouts: 9.02 us -> 3.89 us
    ppermute x8 -> x0, starting transfers between devices: 14.8 us -> none  [the longest x4 9.67 us: exchange(): received.append(lax.ppermute(down, axis, forward))]
    ppermute x8 -> x0, waiting for transfers between devices: 14.1 us -> none  [the longest x4 14.1 us: exchange(): received.append(lax.ppermute(down, axis, forward))]
    pallas_call x2 -> x4, Pallas kernels: 30.6 us -> 44.4 us  [the longest x2 28.9 us: exchange(): pl.pallas_call(functools.partial(halo_kernel, regions, doms), out_shape=j...]
    unnamed x27 -> x15, local copies, waits for them, and re-layouts: 9.02 us -> 3.89 us
  transfers between devices with their start and end apart: 8 -> 0, of which waited for: 2 -> 0; matrix products, arithmetic and copies ran while one was open for 0% -> 0% of each run, Pallas kernels for 0% -> 0%
where the time goes in v2:
time: 128 us; the launch traced here: 127 us
  Pallas kernels  119 us (93%)
  local copies, waits for them, and re-layouts  3.89 us (3%)
  matrix products  2.74 us (2%)
    pallas_call x3, Pallas kernels, all_sum(): pl.pallas_call(functools.partial(reduce_kernel, regions, doms, pieces), o...  49.1 us
    pallas_call x2, Pallas kernels, exchange(): pl.pallas_call(functools.partial(halo_kernel, regions, doms), out_shape=j...  28.9 us
    pallas_call x2, Pallas kernels, graph(): pl.pallas_call(functools.partial(graph_kernel, 1.0 / node_total, 1.0 / ma...  25.9 us
    pallas_call x2, Pallas kernels, inverse_factor(): pl.pallas_call(invert_kernel, out_shape=jax.ShapeDtypeStruct((2 * width,...  15.5 us
    unnamed x15, local copies, waits for them, and re-layouts  3.89 us
    dot_general x1, matrix products, shards(): lax.dot_general(x_init, x_init, (((0,), (0,)), ((), ())), preferred_eleme...  2.74 us

profile of v2, /device:TPU:0, one launch (start us, length us, event | category | flops | bytes accessed | tf_op | source)
XLA Modules:
  0.0 127.5 jit_solution(17444613585539484220)
XLA Ops:
  0.6 0.0 copy-start.4
  0.6 0.0 copy-start
  0.6 2.7 %fusion.x_ref = f32[16,8,128]{2,1,0:T(8,128)} fusion(bf16[4096,128]{1,0:T(8,128)(2,1)} %param.6), kind=kOutput, calls=%fused_computation.1 | convolution fusion | flops 134234112 | bytes 1114112 | tf_op jit(solution)/shard_map/dot_general | solution.py:351
  3.4 0.0 copy-start.5
  3.4 0.0 copy-start.6
  3.4 17.8 %allsum0.1 = f32[16,8,128]{2,1,0:T(8,128)} custom-call(f32[16,8,128]{2,1,0:T(8,128)} %fusion.x_ref), custom_call_target="tpu_custom_call" | custom-call | tf_op jit(solution)/shard_map/allsum0/pallas_call | solution.py:103
  21.2 7.8 %invert.2.both_ref = bf16[256,128]{1,0:T(8,128)(2,1)} custom-call(f32[128,128]{1,0:T(8,128)} %bitcast.15), custom_call_target="tpu_custom_call" | custom-call | tf_op jit(solution)/shard_map/invert/pallas_call | solution.py:177
  28.9 0.0 copy-done.4
  28.9 0.0 copy-done
  28.9 0.0 copy-start.2
  28.9 0.8 copy-done.2
  29.8 14.5 %halo3.1.ext = bf16[64,128,128]{2,1,0:T(8,128)(2,1)S(1)} custom-call(bf16[256,128]{1,0:T(8,128)(2,1)S(1)} %copy-done.2, bf16[32,128,128]{2,1,0:T(8,128)(2,1)S(1)} %bitcast.11, s32[1,4,8]{2,1,0:T(4,128)S(1)} %copy-done.4), custom_call_target="tpu_custom_call" | custom-call | tf_op jit(solution)/shard_map/halo3/pallas_call | solution.py:258
  44.3 0.0 copy-done.5
  44.3 0.0 copy-done.6
  44.3 12.4 %graph.2 = (bf16[32,128,128]{2,1,0:T(8,128)(2,1)S(1)}, f32[128,128]{1,0:T(8,128)S(1)}, f32[128,128]{1,0:T(8,128)S(1)}) custom-call(s32[288]{0:T(512)S(1)} %copy-done.5, s32[288]{0:T(512)S(1)} %copy-done.6, bf16[288,128,128]{2,1,0:T(8,128)(2,1)} %tiles_ref.3, bf16[64,128,128]{2,1,0:T(8,128)(2,1)S(1)} %halo3.1.ext), custom_call_target="tpu_custom_call" | custom-call | tf_op jit(solution)/shard_map/graph/pallas_call | solution.py:324
  56.7 0.0 copy-start.3
  56.7 0.6 copy-done.3
  57.3 14.2 %allsum1.1 = f32[16,8,128]{2,1,0:T(8,128)} custom-call(f32[16,8,128]{2,1,0:T(8,128)} %bitcast.12), custom_call_target="tpu_custom_call" | custom-call | tf_op jit(solution)/shard_map/allsum1/pallas_call | solution.py:103
  71.6 7.8 %invert.3.both_ref = bf16[256,128]{1,0:T(8,128)(2,1)} custom-call(f32[128,128]{1,0:T(8,128)} %bitcast.16), custom_call_target="tpu_custom_call" | custom-call | tf_op jit(solution)/shard_map/invert/pallas_call | solution.py:177
  79.3 0.0 copy-start.1
  79.3 0.8 copy-done.1
  80.2 14.4 %halo4.1.ext = bf16[64,128,128]{2,1,0:T(8,128)(2,1)S(1)} custom-call(bf16[256,128]{1,0:T(8,128)(2,1)S(1)} %copy-done.1, bf16[32,128,128]{2,1,0:T(8,128)(2,1)S(1)} %get-tuple-element.8.cur_ref, s32[1,4,8]{2,1,0:T(4,128)S(1)} %copy-done.4), custom_call_target="tpu_custom_call" | custom-call | tf_op jit(solution)/shard_map/halo4/pallas_call | solution.py:258
  94.6 13.5 %graph.3 = (bf16[32,128,128]{2,1,0:T(8,128)(2,1)}, f32[128,128]{1,0:T(8,128)}, f32[128,128]{1,0:T(8,128)S(1)}) custom-call(s32[288]{0:T(512)S(1)} %copy-done.5, s32[288]{0:T(512)S(1)} %copy-done.6, bf16[288,128,128]{2,1,0:T(8,128)(2,1)} %tiles_ref.3, bf16[64,128,128]{2,1,0:T(8,128)(2,1)S(1)} %halo4.1.ext), custom_call_target="tpu_custom_call" | custom-call | tf_op jit(solution)/shard_map/graph/pallas_call | solution.py:324
  108.1 0.7 pad_maximum_fusion
  108.8 17.1 %allsum2.1 = f32[16,16,128]{2,1,0:T(8,128)} custom-call(f32[16,16,128]{2,1,0:T(8,128)} %bitcast.13), custom_call_target="tpu_custom_call" | custom-call | tf_op jit(solution)/shard_map/allsum2/pallas_call | solution.py:103
  125.9 1.6 %copy.8 = f32[2,128,128]{2,1,0:T(8,128)} copy(f32[2,128,128]{2,1,0:T(8,128)} %bitcast.14) | data formatting | bytes 262144
Async XLA Ops:
  0.6 28.3 %copy-start.4 = (s32[1,4,8]{2,1,0:T(4,128)S(1)}, s32[1,4,8]{2,1,0:T(4,128)}, u32[]{:S(2)}) copy-start(s32[1,4,8]{2,1,0:T(4,128)} %list_ref.3) | copy-start | bytes 388
  0.6 28.3 %copy-start = (bf16[4096,128]{1,0:T(8,128)(2,1)S(1)}, bf16[4096,128]{1,0:T(8,128)(2,1)}, u32[]{:S(2)}) copy-start(bf16[4096,128]{1,0:T(8,128)(2,1)} %param.6) | copy-start | bytes 3145732
  3.4 40.9 %copy-start.5 = (s32[288]{0:T(512)S(1)}, s32[288]{0:T(512)}, u32[]{:S(2)}) copy-start(s32[288]{0:T(512)} %row_ref.3) | copy-start | bytes 3460
  3.4 40.9 %copy-start.6 = (s32[288]{0:T(512)S(1)}, s32[288]{0:T(512)}, u32[]{:S(2)}) copy-start(s32[288]{0:T(512)} %col_ref.3) | copy-start | bytes 3460
  28.9 0.8 copy-start.2
  56.7 0.6 copy-start.3
  79.3 0.8 copy-start.1

commit v3 on v2

--- a/solution.py
+++ b/solution.py
@@ -17,101 +17,79 @@
 LIMIT = 48 * 1024 * 1024
 
 
-def reduce_kernel(regions, doms, pieces, x_ref, o_ref, scat, res, send_a, recv_a, send_b, recv_b):
-    total = regions * doms
-    stride = total // pieces
-    me = lax.axis_index("dom") * regions + lax.axis_index("region")
-    mine = me // stride
-    owner = lax.rem(me, stride) == 0
-
-    def away(off):
-        flat = me + off
-        flat = jnp.where(flat >= total, flat - total, flat)
-        return (lax.rem(flat, regions), flat // regions)
+def reduce_kernel(regions, doms, x_ref, o_ref, part, column, res, send_a, recv_a, send_b, recv_b, send_c, recv_c):
+    region, dom = lax.axis_index("region"), lax.axis_index("dom")
+
+    def across(off):
+        target = region + off
+        return jnp.where(target >= regions, target - regions, target)
+
+    def along(off):
+        target = dom + off
+        return jnp.where(target >= doms, target - doms, target)
 
     barrier = pltpu.get_barrier_semaphore()
-
-    def greet(off, carry):
-        pl.semaphore_signal(
-            barrier, inc=1, device_id=away(off), device_id_type=MESH
-        )
-        return carry
-
-    lax.fori_loop(1, total, greet, 0)
-    pl.semaphore_wait(barrier, total - 1)
-
-    def scatter(step, carry):
-        piece = lax.rem(mine + step, pieces)
-        target = piece * stride
-
-        @pl.when(target != me)
-        def _():
-            pltpu.make_async_remote_copy(
-                src_ref=x_ref.at[piece],
-                dst_ref=scat.at[lax.rem(me - target - 1 + total, total)],
-                send_sem=send_a,
-                recv_sem=recv_a,
-                device_id=(lax.rem(target, regions), target // regions),
-                device_id_type=MESH,
-            ).start()
-
-        return carry
-
-    lax.fori_loop(0, pieces, scatter, 0)
-
-    @pl.when(owner)
-    def _():
-        pltpu.make_async_copy(scat, scat, recv_a).wait()
-        parts = [scat[s] for s in range(total - 1)] + [x_ref[mine]]
-        while len(parts) > 1:
-            parts = [a + b for a, b in zip(parts[::2], parts[1::2])] + (
-                [parts[-1]] if len(parts) % 2 else []
-            )
-        res[mine] = parts[0]
-
-        def spread(off, carry):
-            pltpu.make_async_remote_copy(
-                src_ref=res.at[mine],
-                dst_ref=res.at[mine],
-                send_sem=send_b,
-                recv_sem=recv_b,
-                device_id=away(off),
-                device_id_type=MESH,
-            ).start()
-            return carry
-
-        lax.fori_loop(1, total, spread, 0)
-        rest = res.at[pl.ds(0, pieces - 1)]
-        pltpu.make_async_copy(rest, rest, recv_b).wait()
-        sent = x_ref.at[pl.ds(0, pieces - 1)]
-        pltpu.make_async_copy(sent, sent, send_a).wait()
-        pltpu.make_async_copy(scat, scat, send_b).wait()
-
-    @pl.when(jnp.logical_not(owner))
-    def _():
-        pltpu.make_async_copy(res, res, recv_b).wait()
-        pltpu.make_async_copy(x_ref, x_ref, send_a).wait()
-
+    for off in range(1, regions):
+        pl.semaphore_signal(barrier, inc=1, device_id=(across(off), dom), device_id_type=MESH)
+    for off in range(1, doms):
+        pl.semaphore_signal(barrier, inc=1, device_id=(region, along(off)), device_id_type=MESH)
+    part[region] = x_ref[region]
+    pl.semaphore_wait(barrier, regions + doms - 2)
+
+    def send(src, dst, sems, off, target):
+        copy = pltpu.make_async_remote_copy(
+            src_ref=src,
+            dst_ref=dst,
+            send_sem=sems[0].at[off - 1],
+            recv_sem=sems[1].at[off - 1],
+            device_id=target,
+            device_id_type=MESH,
+        )
+        copy.start()
+        return copy
+
+    first = [
+        send(x_ref.at[across(o)], part.at[region], (send_a, recv_a), o, (across(o), dom))
+        for o in range(1, regions)
+    ]
+    for copy in first:
+        copy.wait_recv()
+    column[dom] = jnp.sum(part[...], axis=0)
+    second = [
+        send(column.at[dom], column.at[dom], (send_b, recv_b), o, (region, along(o)))
+        for o in range(1, doms)
+    ]
+    for copy in second:
+        copy.wait_recv()
+    res[region] = jnp.sum(column[...], axis=0)
+    third = [
+        send(res.at[region], res.at[region], (send_c, recv_c), o, (across(o), dom))
+        for o in range(1, regions)
+    ]
+    for copy in third:
+        copy.wait_recv()
     o_ref[...] = res[...]
+    for copy in first + second + third:
+        copy.wait_send()
 
 
 def all_sum(x, regions, doms, ident):
     rows, lanes = x.shape
-    total = regions * doms
-    pieces = min(total, 16)
-    shape = (pieces, rows // pieces, lanes)
+    piece = (rows // regions, lanes)
+    shape = (regions,) + piece
     out = pl.pallas_call(
-        functools.partial(reduce_kernel, regions, doms, pieces),
+        functools.partial(reduce_kernel, regions, doms),
         out_shape=jax.ShapeDtypeStruct(shape, F32),
         in_specs=[VM],
         out_specs=VM,
         scratch_shapes=[
-            pltpu.VMEM((total - 1,) + shape[1:], F32),
             pltpu.VMEM(shape, F32),
-            pltpu.SemaphoreType.DMA,
-            pltpu.SemaphoreType.DMA,
-            pltpu.SemaphoreType.DMA,
-            pltpu.SemaphoreType.DMA,
+            pltpu.VMEM((doms,) + piece, F32),
+            pltpu.VMEM(shape, F32),
+        ]
+        + [
+            pltpu.SemaphoreType.DMA((count - 1,))
+            for count in (regions, regions, doms, doms, regions, regions)
         ],
         compiler_params=pltpu.CompilerParams(collective_id=ident, has_side_effects=True),
         name="allsum" + str(ident),

time: 128 us -> 131 us (1.023)
  Pallas kernels: 119 us -> 122 us
    pallas_call x3, Pallas kernels: 49.1 us -> 51.4 us  [all_sum(): pl.pallas_call(functools.partial(reduce_kernel, regions, doms), out_shape...]
where the time goes in v3:
time: 131 us; the launch traced here: 130 us
  Pallas kernels  122 us (93%)
  local copies, waits for them, and re-layouts  3.89 us (3%)
  matrix products  2.74 us (2%)
    pallas_call x3, Pallas kernels, all_sum(): pl.pallas_call(functools.partial(reduce_kernel, regions, doms), out_shape...  51.4 us
    pallas_call x2, Pallas kernels, exchange(): pl.pallas_call(functools.partial(halo_kernel, regions, doms), out_shape=j...  29 us
    pallas_call x2, Pallas kernels, graph(): pl.pallas_call(functools.partial(graph_kernel, 1.0 / node_total, 1.0 / ma...  25.9 us
    pallas_call x2, Pallas kernels, inverse_factor(): pl.pallas_call(invert_kernel, out_shape=jax.ShapeDtypeStruct((2 * width,...  15.5 us
    unnamed x15, local copies, waits for them, and re-layouts  3.89 us
    dot_general x1, matrix products, shards(): lax.dot_general(x_init, x_init, (((0,), (0,)), ((), ())), preferred_eleme...  2.74 us

profile of v3, /device:TPU:0, one launch (start us, length us, event | category | flops | bytes accessed | tf_op | source)
XLA Modules:
  0.0 129.9 jit_solution(18102818108220030487)
XLA Ops:
  0.6 0.0 copy-start.4
  0.6 0.0 copy-start
  0.6 2.7 %convolution_multiply_fusion = f32[128,128]{1,0:T(8,128)} fusion(bf16[4096,128]{1,0:T(8,128)(2,1)} %param.6), kind=kOutput, calls=%fused_computation | convolution fusion | flops 134234112 | bytes 1114112 | tf_op jit(solution)/shard_map/dot_general | solution.py:329
  3.4 0.0 copy-start.5
  3.4 0.0 copy-start.6
  3.4 16.7 %allsum0.1 = f32[4,32,128]{2,1,0:T(8,128)} custom-call(f32[4,32,128]{2,1,0:T(8,128)} %bitcast.14), custom_call_target="tpu_custom_call" | custom-call | tf_op jit(solution)/shard_map/allsum0/pallas_call | solution.py:80
  20.1 7.8 %invert.2.both_ref = bf16[256,128]{1,0:T(8,128)(2,1)} custom-call(f32[128,128]{1,0:T(8,128)} %bitcast.15), custom_call_target="tpu_custom_call" | custom-call | tf_op jit(solution)/shard_map/invert/pallas_call | solution.py:155
  27.8 0.0 copy-done.4
  27.8 0.0 copy-done
  27.8 0.0 copy-start.2
  27.8 0.8 copy-done.2
  28.7 14.5 %halo3.1.ext = bf16[64,128,128]{2,1,0:T(8,128)(2,1)S(1)} custom-call(bf16[256,128]{1,0:T(8,128)(2,1)S(1)} %copy-done.2, bf16[32,128,128]{2,1,0:T(8,128)(2,1)S(1)} %bitcast.10, s32[1,4,8]{2,1,0:T(4,128)S(1)} %copy-done.4), custom_call_target="tpu_custom_call" | custom-call | tf_op jit(solution)/shard_map/halo3/pallas_call | solution.py:236
  43.2 0.0 copy-done.5
  43.2 0.0 copy-done.6
  43.2 12.4 %graph.2 = (bf16[32,128,128]{2,1,0:T(8,128)(2,1)S(1)}, f32[128,128]{1,0:T(8,128)S(1)}, f32[128,128]{1,0:T(8,128)S(1)}) custom-call(s32[288]{0:T(512)S(1)} %copy-done.5, s32[288]{0:T(512)S(1)} %copy-done.6, bf16[288,128,128]{2,1,0:T(8,128)(2,1)} %tiles_ref.3, bf16[64,128,128]{2,1,0:T(8,128)(2,1)S(1)} %halo3.1.ext), custom_call_target="tpu_custom_call" | custom-call | tf_op jit(solution)/shard_map/graph/pallas_call | solution.py:302
  55.6 0.0 copy-start.3
  55.6 0.6 copy-done.3
  56.3 16.7 %allsum1.1 = f32[4,32,128]{2,1,0:T(8,128)} custom-call(f32[4,32,128]{2,1,0:T(8,128)} %bitcast.11), custom_call_target="tpu_custom_call" | custom-call | tf_op jit(solution)/shard_map/allsum1/pallas_call | solution.py:80
  72.9 7.8 %invert.3.both_ref = bf16[256,128]{1,0:T(8,128)(2,1)} custom-call(f32[128,128]{1,0:T(8,128)} %bitcast.16), custom_call_target="tpu_custom_call" | custom-call | tf_op jit(solution)/shard_map/invert/pallas_call | solution.py:155
  80.7 0.0 copy-start.1
  80.7 0.8 copy-done.1
  81.5 14.5 %halo4.1.ext = bf16[64,128,128]{2,1,0:T(8,128)(2,1)S(1)} custom-call(bf16[256,128]{1,0:T(8,128)(2,1)S(1)} %copy-done.1, bf16[32,128,128]{2,1,0:T(8,128)(2,1)S(1)} %get-tuple-element.8.cur_ref, s32[1,4,8]{2,1,0:T(4,128)S(1)} %copy-done.4), custom_call_target="tpu_custom_call" | custom-call | tf_op jit(solution)/shard_map/halo4/pallas_call | solution.py:236
  96.0 13.5 %graph.3 = (bf16[32,128,128]{2,1,0:T(8,128)(2,1)}, f32[128,128]{1,0:T(8,128)}, f32[128,128]{1,0:T(8,128)S(1)}) custom-call(s32[288]{0:T(512)S(1)} %copy-done.5, s32[288]{0:T(512)S(1)} %copy-done.6, bf16[288,128,128]{2,1,0:T(8,128)(2,1)} %tiles_ref.3, bf16[64,128,128]{2,1,0:T(8,128)(2,1)S(1)} %halo4.1.ext), custom_call_target="tpu_custom_call" | custom-call | tf_op jit(solution)/shard_map/graph/pallas_call | solution.py:302
  109.6 0.7 pad_maximum_fusion
  110.2 18.1 %allsum2.1 = f32[4,64,128]{2,1,0:T(8,128)} custom-call(f32[4,64,128]{2,1,0:T(8,128)} %bitcast.12), custom_call_target="tpu_custom_call" | custom-call | tf_op jit(solution)/shard_map/allsum2/pallas_call | solution.py:80
  128.3 1.6 %copy.8 = f32[2,128,128]{2,1,0:T(8,128)} copy(f32[2,128,128]{2,1,0:T(8,128)} %bitcast.13) | data formatting | bytes 262144
Async XLA Ops:
  0.6 27.2 %copy-start.4 = (s32[1,4,8]{2,1,0:T(4,128)S(1)}, s32[1,4,8]{2,1,0:T(4,128)}, u32[]{:S(2)}) copy-start(s32[1,4,8]{2,1,0:T(4,128)} %list_ref.3) | copy-start | bytes 388
  0.6 27.2 %copy-start = (bf16[4096,128]{1,0:T(8,128)(2,1)S(1)}, bf16[4096,128]{1,0:T(8,128)(2,1)}, u32[]{:S(2)}) copy-start(bf16[4096,128]{1,0:T(8,128)(2,1)} %param.6) | copy-start | bytes 3145732
  3.4 39.8 %copy-start.5 = (s32[288]{0:T(512)S(1)}, s32[288]{0:T(512)}, u32[]{:S(2)}) copy-start(s32[288]{0:T(512)} %row_ref.3) | copy-start | bytes 3460
  3.4 39.8 %copy-start.6 = (s32[288]{0:T(512)S(1)}, s32[288]{0:T(512)}, u32[]{:S(2)}) copy-start(s32[288]{0:T(512)} %col_ref.3) | copy-start | bytes 3460
  27.8 0.8 copy-start.2
  55.6 0.6 copy-start.3
  80.7 0.8 copy-start.1

commit v4 on v2

--- a/solution.py
+++ b/solution.py
@@ -284,10 +284,14 @@
     def _():
         acc[...] = jnp.zeros_like(acc)
 
-    for t in range(group):
-        row = row_ref[step * group + t]
-        col = col_ref[step * group + t]
-        acc[row] += jnp.dot(tiles_ref[t], ext[col], preferred_element_type=F32)
+    for start in range(0, group, 2):
+        batch = range(start, min(start + 2, group))
+        products = [
+            jnp.dot(tiles_ref[t], ext[col_ref[step * group + t]], preferred_element_type=F32)
+            for t in batch
+        ]
+        for t, product in zip(batch, products):
+            acc[row_ref[step * group + t]] += product
 
     @pl.when(step == pl.num_programs(0) - 1)
     def _():

time: 128 us -> 128 us (level)
  no operation moved by 1% of the time
where the time goes in v4:
time: 128 us; the launch traced here: 127 us
  Pallas kernels  119 us (93%)
  local copies, waits for them, and re-layouts  3.89 us (3%)
  matrix products  2.74 us (2%)
    pallas_call x3, Pallas kernels, all_sum(): pl.pallas_call(functools.partial(reduce_kernel, regions, doms, pieces), o...  49.1 us
    pallas_call x2, Pallas kernels, exchange(): pl.pallas_call(functools.partial(halo_kernel, regions, doms), out_shape=j...  28.9 us
    pallas_call x2, Pallas kernels, graph(): pl.pallas_call(functools.partial(graph_kernel, 1.0 / node_total, 1.0 / ma...  25.9 us
    pallas_call x2, Pallas kernels, inverse_factor(): pl.pallas_call(invert_kernel, out_shape=jax.ShapeDtypeStruct((2 * width,...  15.5 us
    unnamed x15, local copies, waits for them, and re-layouts  3.89 us
    dot_general x1, matrix products, shards(): lax.dot_general(x_init, x_init, (((0,), (0,)), ((), ())), preferred_eleme...  2.74 us

profile of v4, /device:TPU:0, one launch (start us, length us, event | category | flops | bytes accessed | tf_op | source)
XLA Modules:
  0.0 127.5 jit_solution(4448433346614707483)
XLA Ops:
  0.6 0.0 copy-start.4
  0.6 0.0 copy-start
  0.6 2.7 %fusion.x_ref = f32[16,8,128]{2,1,0:T(8,128)} fusion(bf16[4096,128]{1,0:T(8,128)(2,1)} %param.6), kind=kOutput, calls=%fused_computation.1 | convolution fusion | flops 134234112 | bytes 1114112 | tf_op jit(solution)/shard_map/dot_general | solution.py:355
  3.4 0.0 copy-start.5
  3.4 0.0 copy-start.6
  3.4 17.8 %allsum0.1 = f32[16,8,128]{2,1,0:T(8,128)} custom-call(f32[16,8,128]{2,1,0:T(8,128)} %fusion.x_ref), custom_call_target="tpu_custom_call" | custom-call | tf_op jit(solution)/shard_map/allsum0/pallas_call | solution.py:103
  21.2 7.8 %invert.2.both_ref = bf16[256,128]{1,0:T(8,128)(2,1)} custom-call(f32[128,128]{1,0:T(8,128)} %bitcast.15), custom_call_target="tpu_custom_call" | custom-call | tf_op jit(solution)/shard_map/invert/pallas_call | solution.py:177
  28.9 0.0 copy-done.4
  28.9 0.0 copy-done
  28.9 0.0 copy-start.2
  28.9 0.8 copy-done.2
  29.8 14.5 %halo3.1.ext = bf16[64,128,128]{2,1,0:T(8,128)(2,1)S(1)} custom-call(bf16[256,128]{1,0:T(8,128)(2,1)S(1)} %copy-done.2, bf16[32,128,128]{2,1,0:T(8,128)(2,1)S(1)} %bitcast.11, s32[1,4,8]{2,1,0:T(4,128)S(1)} %copy-done.4), custom_call_target="tpu_custom_call" | custom-call | tf_op jit(solution)/shard_map/halo3/pallas_call | solution.py:258
  44.3 0.0 copy-done.5
  44.3 0.0 copy-done.6
  44.3 12.4 %graph.2 = (bf16[32,128,128]{2,1,0:T(8,128)(2,1)S(1)}, f32[128,128]{1,0:T(8,128)S(1)}, f32[128,128]{1,0:T(8,128)S(1)}) custom-call(s32[288]{0:T(512)S(1)} %copy-done.5, s32[288]{0:T(512)S(1)} %copy-done.6, bf16[288,128,128]{2,1,0:T(8,128)(2,1)} %tiles_ref.3, bf16[64,128,128]{2,1,0:T(8,128)(2,1)S(1)} %halo3.1.ext), custom_call_target="tpu_custom_call" | custom-call | tf_op jit(solution)/shard_map/graph/pallas_call | solution.py:328
  56.7 0.0 copy-start.3
  56.7 0.6 copy-done.3
  57.3 14.2 %allsum1.1 = f32[16,8,128]{2,1,0:T(8,128)} custom-call(f32[16,8,128]{2,1,0:T(8,128)} %bitcast.12), custom_call_target="tpu_custom_call" | custom-call | tf_op jit(solution)/shard_map/allsum1/pallas_call | solution.py:103
  71.6 7.8 %invert.3.both_ref = bf16[256,128]{1,0:T(8,128)(2,1)} custom-call(f32[128,128]{1,0:T(8,128)} %bitcast.16), custom_call_target="tpu_custom_call" | custom-call | tf_op jit(solution)/shard_map/invert/pallas_call | solution.py:177
  79.3 0.0 copy-start.1
  79.3 0.8 copy-done.1
  80.2 14.4 %halo4.1.ext = bf16[64,128,128]{2,1,0:T(8,128)(2,1)S(1)} custom-call(bf16[256,128]{1,0:T(8,128)(2,1)S(1)} %copy-done.1, bf16[32,128,128]{2,1,0:T(8,128)(2,1)S(1)} %get-tuple-element.8.cur_ref, s32[1,4,8]{2,1,0:T(4,128)S(1)} %copy-done.4), custom_call_target="tpu_custom_call" | custom-call | tf_op jit(solution)/shard_map/halo4/pallas_call | solution.py:258
  94.6 13.5 %graph.3 = (bf16[32,128,128]{2,1,0:T(8,128)(2,1)}, f32[128,128]{1,0:T(8,128)}, f32[128,128]{1,0:T(8,128)S(1)}) custom-call(s32[288]{0:T(512)S(1)} %copy-done.5, s32[288]{0:T(512)S(1)} %copy-done.6, bf16[288,128,128]{2,1,0:T(8,128)(2,1)} %tiles_ref.3, bf16[64,128,128]{2,1,0:T(8,128)(2,1)S(1)} %halo4.1.ext), custom_call_target="tpu_custom_call" | custom-call | tf_op jit(solution)/shard_map/graph/pallas_call | solution.py:328
  108.1 0.7 pad_maximum_fusion
  108.8 17.1 %allsum2.1 = f32[16,16,128]{2,1,0:T(8,128)} custom-call(f32[16,16,128]{2,1,0:T(8,128)} %bitcast.13), custom_call_target="tpu_custom_call" | custom-call | tf_op jit(solution)/shard_map/allsum2/pallas_call | solution.py:103
  125.9 1.6 %copy.8 = f32[2,128,128]{2,1,0:T(8,128)} copy(f32[2,128,128]{2,1,0:T(8,128)} %bitcast.14) | data formatting | bytes 262144
Async XLA Ops:
  0.6 28.3 %copy-start.4 = (s32[1,4,8]{2,1,0:T(4,128)S(1)}, s32[1,4,8]{2,1,0:T(4,128)}, u32[]{:S(2)}) copy-start(s32[1,4,8]{2,1,0:T(4,128)} %list_ref.3) | copy-start | bytes 388
  0.6 28.3 %copy-start = (bf16[4096,128]{1,0:T(8,128)(2,1)S(1)}, bf16[4096,128]{1,0:T(8,128)(2,1)}, u32[]{:S(2)}) copy-start(bf16[4096,128]{1,0:T(8,128)(2,1)} %param.6) | copy-start | bytes 3145732
  3.4 40.9 %copy-start.5 = (s32[288]{0:T(512)S(1)}, s32[288]{0:T(512)}, u32[]{:S(2)}) copy-start(s32[288]{0:T(512)} %row_ref.3) | copy-start | bytes 3460
  3.4 40.9 %copy-start.6 = (s32[288]{0:T(512)S(1)}, s32[288]{0:T(512)}, u32[]{:S(2)}) copy-start(s32[288]{0:T(512)} %col_ref.3) | copy-start | bytes 3460
  28.9 0.8 copy-start.2
  56.7 0.6 copy-start.3
  79.3 0.8 copy-start.1
